TPU v7x, 768 devices: a whole 4x8x12 slice. The times are simulated.
768 devices in a mesh: row: 16 (over x_lo, y), col: 48 (over x_hi, z, core).
Axes of the slice: x: 4 (x_hi: 2, x_lo: 2; x = x_hi * 2 + x_lo), y: 8, z: 12, core: 2. Of those that a mesh axis runs over, the one named last changes fastest.
Arguments:
- features: bfloat16 [98304, 128], P(('row', 'col')), may hold values from -6 to 6
- node_scale: bfloat16 [98304], P(('row', 'col')), may hold values from 0.099609375 to 0.29882812
- weight: bfloat16 [128, 256], replicated, may hold values from -0.5 to 0.5
- bias: float32 [256], replicated, may hold values from -3 to 3
- block_rows: int32 [16, 48, 16], P('row', 'col'), may hold values from 0 to 47, as said below
- block_cols: int32 [16, 48, 16], P('row', 'col'), may hold values from 0 to 15
- block_masks: int32 [16, 48, 16, 128, 128], P('row', 'col'), may hold values from 0 to 1, as said below
- out_grad: bfloat16 [98304, 256], P(('row', 'col')), may hold values from -6 to 6
Outputs:
- hidden: bfloat16 [98304, 256], P(('row', 'col'))
- grad_features: bfloat16 [98304, 128], P(('row', 'col'))
- grad_weight: float32 [128, 256], replicated
- grad_bias: float32 [256], replicated
Inputs may be any that keep to these rules, and one draw needn't show every extreme that they name: `block_rows`: on each device, slot s names entry s % 48 of an ordering of the tile's 48 block rows, so a block row repeats only after all have been named; repeated blocks add their edges. `block_masks`: on each device the slots that hold edges come first, at least 8 of them, and the rest are all zero; at least one device has edges in all 16 slots.
All inputs are finite; a program needn't handle non-finite values.
Results may differ from a plain program's by a relative error of at most 0.007.
Values may be sent and summed in bfloat16 or wider, within the bound.
A program may use at most 32 MiB of HBM per device.

v0:
```python
import jax
import jax.numpy as jnp
from jax import lax
from jax.sharding import PartitionSpec as P


def activation(value):
    return jax.nn.gelu(value, approximate=True)


def place_blocks(contrib, coords, total_blocks):
    selector = (coords[None, :] == jnp.arange(total_blocks, dtype=jnp.int32)[:, None]).astype(
        jnp.float32
    )
    return jnp.einsum("bs,sif->bif", selector, contrib, precision=lax.Precision.HIGHEST)


def on_device(features, node_scale, weight, bias, block_rows, block_cols, block_masks, out_grad):
    rows_here = features.shape[0]
    feature_width = features.shape[1]
    block_size = block_masks.shape[-1]
    slot_count = block_masks.shape[2]
    col_count = lax.axis_size("col")
    masks = block_masks.reshape(slot_count, block_size, block_size).astype(jnp.bfloat16)
    row_ids = block_rows.reshape(slot_count)
    col_ids = block_cols.reshape(slot_count)
    scale_col = node_scale.astype(jnp.float32)[:, None]
    scaled = (scale_col * features.astype(jnp.float32)).astype(jnp.bfloat16)
    column_group = lax.all_gather(scaled, "row", axis=0, tiled=True)
    picked = column_group.reshape(-1, block_size, feature_width)[col_ids]
    products = jnp.einsum("sij,sjf->sif", masks, picked, preferred_element_type=jnp.float32)
    tile_row_blocks = col_count * rows_here // block_size
    partial_value = place_blocks(products, row_ids, tile_row_blocks).reshape(-1, feature_width)
    summed = lax.psum_scatter(partial_value, "col", scatter_dimension=0, tiled=True)
    aggregated = (scale_col * summed).astype(jnp.bfloat16)
    preact = jnp.dot(aggregated, weight, preferred_element_type=jnp.float32) + bias
    active, pullback = jax.vjp(activation, preact)
    hidden = active.astype(jnp.bfloat16)
    grad_pre = pullback(out_grad.astype(jnp.float32))[0].astype(jnp.bfloat16)
    weight_part = lax.dot_general(
        aggregated, grad_pre, (((0,), (0,)), ((), ())), preferred_element_type=jnp.float32
    )
    bias_part = jnp.sum(grad_pre.astype(jnp.float32), axis=0)
    grad_weight, grad_bias = lax.psum((weight_part, bias_part), ("row", "col"))
    grads_all, scales_all = (
        lax.all_gather(grad_pre, "col", axis=0, tiled=True),
        lax.all_gather(node_scale, "col", axis=0, tiled=True),
    )
    row_group = (
        scales_all.astype(jnp.float32)[:, None]
        * jnp.dot(grads_all, weight.T, preferred_element_type=jnp.float32)
    ).astype(jnp.bfloat16)
    chosen = row_group.reshape(-1, block_size, feature_width)[row_ids]
    back_terms = jnp.einsum("sij,sif->sjf", masks, chosen, preferred_element_type=jnp.float32)
    tile_col_blocks = lax.axis_size("row") * rows_here // block_size
    partial_back = place_blocks(back_terms, col_ids, tile_col_blocks).reshape(-1, feature_width)
    summed_back = lax.psum_scatter(partial_back, "row", scatter_dimension=0, tiled=True)
    grad_features = (scale_col * summed_back).astype(jnp.bfloat16)
    return (hidden, grad_features, grad_weight, grad_bias)


def solution(mesh):
    return jax.shard_map(
        on_device,
        mesh=mesh,
        in_specs=(
            P(("row", "col"), None),
            P(("row", "col")),
            P(),
            P(),
            P("row", "col", None),
            P("row", "col", None),
            P("row", "col", None, None, None),
            P(("row", "col"), None),
        ),
        out_specs=(P(("row", "col"), None), P(("row", "col"), None), P(), P()),
        check_vma=False,
    )
```

profile of v0, /device:TPU:1, one launch (start us, length us, event | category | flops | bytes accessed | tf_op | source)
XLA Modules:
  0.0 932.9 jit_solution(8809352855861246096)
XLA Ops:
  7.2 0.7 convert_element_type.41
  7.9 0.8 multiply_convert_fusion.3
  8.7 30.6 %all_gather.9 = bf16[2048,128]{1,0:T(8,128)(2,1)S(1)} all-gather(bf16[128,128]{1,0:T(8,128)(2,1)S(1)} %multiply_convert_fusion.3), channel_id=1, replica_groups=mesh['row'=16,'col'=48] {'row'}, dimensions={0}, use_global_device_ids=true | all-gather | bytes 557056 | tf_op jit(solution)/shard_map/all_gather | solution.py:29
  39.4 0.7 fusion.23
  40.0 0.6 gather_fusion
  40.7 1.7 convolution_bitcast_fusion.1
  42.4 0.5 copy.19
  43.0 1.5 fusion.16
  44.5 2.6 copy.20
  47.2 180.2 %reduce-scatter.3.cloned.1.call-done = f32[128,128]{1,0:T(8,128)} async-done(((f32[6144,128]{1,0:T(8,128)}), f32[128,128]{1,0:T(8,128)}) %reduce-scatter.3.cloned.1.call-update) | async-done | bytes 65552 | tf_op jit(solution)/shard_map/reduce_scatter | solution.py:34
  227.4 1.8 convert_reduce_fusion
  229.2 64.8 %all-gather = bf16[48,1,128]{2,1,0:T(2,128)(2,1)S(1)} all-gather(bf16[1,1,128]{2,1,0:T(2,128)(2,1)S(1)} %bitcast.46), channel_id=1, replica_groups=mesh['row'=16,'col'=48] {'col'}, dimensions={0}, use_global_device_ids=true | all-gather | bytes 12544 | tf_op jit(solution)/shard_map/all_gather | solution.py:47
  294.1 65.8 %all-gather.3.cloned.1.call-done = bf16[6144,256]{1,0:T(8,128)(2,1)} async-done(((bf16[128,256]{1,0:T(8,128)(2,1)}), bf16[6144,256]{1,0:T(8,128)(2,1)}) %all-gather.3.cloned.1.call-update) | async-done | bytes 3145744 | tf_op jit(solution)/shard_map/all_gather | solution.py:46
  359.8 3.0 fusion
  362.8 0.6 gather_fusion.1
  363.5 0.4 convolution_bitcast_fusion
  363.8 0.5 copy.22
  364.4 0.6 fusion.19
  365.0 1.3 copy.23
  366.4 107.0 %psum.15 = f32[256]{0:T(256)} all-reduce(f32[256]{0:T(256)S(1)} %get-tuple-element.4), channel_id=1, replica_groups=mesh['row'=16,'col'=48] {'row','col'}, use_global_device_ids=true, to_apply=%region_4.0 | all-reduce | flops 256 | bytes 2048 | tf_op jit(solution)/shard_map/psum | solution.py:44
  473.3 0.9 fusion.25
  474.3 1.5 multiply_convert_fusion.1
  475.8 449.0 %all-reduce.2.cloned.1.call-done = f32[128,256]{1,0:T(8,128)} async-done(((f32[128,256]{1,0:T(8,128)}), f32[128,256]{1,0:T(8,128)}) %all-reduce.2.cloned.1.call-update) | async-done | bytes 131088 | tf_op jit(solution)/shard_map/psum | solution.py:44
  924.8 1.6 copy.27
  (31 shorter events, 0.3 us)
Async XLA Ops:
  7.2 220.2 %copy-start = (bf16[128,256]{1,0:T(8,128)(2,1)S(1)}, bf16[128,256]{1,0:T(8,128)(2,1)}, u32[]{:S(2)}) copy-start(bf16[128,256]{1,0:T(8,128)(2,1)} %param.10) | copy-start | bytes 196612
  7.2 220.2 %reduce-scatter.3.cloned.1.call-start = ((), (), s32[]{:S(2)}) async-start(), calls=%async_computation.2 | async-start | bytes 3211264 | tf_op jit(solution)/shard_map/reduce_scatter | solution.py:34
  8.7 34.2 %copy-start.4 = (s32[1,1,16]{2,1,0:T(1,128)S(1)}, s32[1,1,16]{2,1,0:T(1,128)}, u32[]{:S(2)}) copy-start(s32[1,1,16]{2,1,0:T(1,128)} %param.12) | copy-start | bytes 196
  47.1 180.3 %copy-start.7 = (bf16[128,256]{1,0:T(8,128)(2,1)S(1)}, bf16[128,256]{1,0:T(8,128)(2,1)}, u32[]{:S(2)}) copy-start(bf16[128,256]{1,0:T(8,128)(2,1)} %param.15) | copy-start | bytes 196612
  47.1 180.3 %copy-start.8 = (f32[256]{0:T(256)S(1)}, f32[256]{0:T(256)}, u32[]{:S(2)}) copy-start(f32[256]{0:T(256)} %param.11) | copy-start | bytes 3076
  47.1 182.1 %copy-start.6 = (bf16[128]{0:T(256)(128)(2,1)S(1)}, bf16[128]{0:T(256)(128)(2,1)}, u32[]{:S(2)}) copy-start(bf16[128]{0:T(256)(128)(2,1)} %param.9) | copy-start | bytes 772
  47.1 312.7 %all-gather.3.cloned.1.call-start = ((), (), s32[]{:S(2)}) async-start(), calls=%async_computation.3 | async-start | bytes 3211264 | tf_op jit(solution)/shard_map/all_gather | solution.py:46
  229.2 245.1 %reduce-scatter.5.cloned.1.call-start = ((), (), s32[]{:S(2)}) async-start(), calls=%async_computation.4 | async-start | bytes 1114112 | tf_op jit(solution)/shard_map/reduce_scatter | solution.py:57
  359.8 3.6 copy-start.1
  362.8 1.6 copy-start.5
  364.3 109.0 %copy-start.2 = (bf16[128,256]{1,0:T(8,128)(2,1)S(1)}, bf16[128,256]{1,0:T(8,128)(2,1)}, u32[]{:S(2)}) copy-start(bf16[128,256]{1,0:T(8,128)(2,1)} %get-tuple-element.5) | copy-start | bytes 196612
  364.4 109.0 %copy-start.3 = (f32[128,128]{1,0:T(8,128)S(1)}, f32[128,128]{1,0:T(8,128)}, u32[]{:S(2)}) copy-start(f32[128,128]{1,0:T(8,128)} %reduce-scatter.3.cloned.1.call-done) | copy-start | bytes 196612
  366.3 558.5 %all-reduce.2.cloned.1.call-start = ((), (), s32[]{:S(2)}) async-start(), calls=%async_computation.5 | async-start | bytes 262144 | tf_op jit(solution)/shard_map/psum | solution.py:44
Sparse Core Ops, SparseCore 0:
  47.2 180.0 reduce-scatter.2
  231.6 128.1 all-gather.2
  366.4 61.1 reduce-scatter.4
  474.4 450.3 all-reduce.1
where the time goes:
time: 934 us; the launch traced here: 933 us
  waiting for transfers between devices  695 us (74%)
  blocking collectives  202 us (22%)
  between operations  13.9 us (1%)
  matrix products  9.9 us (1%)
    psum x1, waiting for transfers between devices, on_device(): grad_weight, grad_bias = lax.psum((weight_part, bias_part), ('row', 'col'))  449 us
    reduce_scatter x1, waiting for transfers between devices, on_device(): lax.psum_scatter(partial_value, 'col', scatter_dimension=0, tiled=True)  180 us
    psum x1, blocking collectives, on_device(): grad_weight, grad_bias = lax.psum((weight_part, bias_part), ('row', 'col'))  107 us
    all_gather x1, waiting for transfers between devices, on_device(): lax.all_gather(grad_pre, 'col', axis=0, tiled=True)  65.8 us
    all_gather x1, blocking collectives, on_device(): lax.all_gather(node_scale, 'col', axis=0, tiled=True)  64.8 us
    all_gather x1, blocking collectives, on_device(): column_group = lax.all_gather(scaled, 'row', axis=0, tiled=True)  30.6 us
  transfers between devices with their start and end apart: 4, of which 3 were waited for; matrix products, arithmetic and copies ran while one was open for 0% of the time, Pallas kernels for 0%

commit v1 on v0

v1 whole, which is shorter than its diff:
```python
import functools
import math

import jax
import jax.numpy as jnp
from jax import lax
from jax.experimental import pallas as pl
from jax.experimental.pallas import tpu as pltpu
from jax.sharding import PartitionSpec as P

MESH = pl.DeviceIdType.MESH
UP, DOWN = 0, 1


def kernel(
    ny, nz,
    table, scale_ref, features_ref, weight_ref, bias_ref, masks_ref, cotangent_ref,
    hidden_ref, grad_features_ref, grad_weight_ref, grad_bias_ref,
    masks, masks_t, gathered, products, pair_out, pair_in, ring_out, ring_in, edge_out, edge_in,
    messages, back, back_out, back_in, back_edge_out, back_edge_in,
    parts, parts_in, halves, y_in, x_terms, z_terms, finals,
    send_sems, recv_sems,
):
    f32, bf16 = jnp.float32, jnp.bfloat16
    slots = masks.shape[0]
    row, col = lax.axis_index("row"), lax.axis_index("col")
    xl, y = row // ny, row % ny
    xh, z, core = col // (2 * nz), (col % (2 * nz)) // 2, col % 2

    def row_of(x_lo, y_at):
        return x_lo * ny + y_at

    def col_of(x_hi, z_at, core_at):
        return x_hi * (2 * nz) + z_at * 2 + core_at

    sibling = (row, col_of(xh, z, 1 - core))
    lo_partner = (row_of(1 - xl, y), col)
    hi_partner = (row, col_of(1 - xh, z, core))
    far_partner = (row_of(1 - xl, y), col_of(1 - xh, z, core))
    y_peers = [(row_of(xl, (y + j) % ny), col) for j in range(1, ny)]
    z_peers = [(row, col_of(xh, (z + j) % nz, core)) for j in range(1, nz)]

    barrier = pltpu.get_barrier_semaphore()
    everyone = [sibling, lo_partner, hi_partner, far_partner] + y_peers + z_peers
    for peer in everyone:
        pl.semaphore_signal(barrier, inc=1, device_id=peer, device_id_type=MESH)

    started = []

    def send(src, dst, peer):
        number = len(started)
        copy = pltpu.make_async_remote_copy(
            src_ref=src, dst_ref=dst, send_sem=send_sems.at[number], recv_sem=recv_sems.at[number],
            device_id=peer, device_id_type=MESH,
        )
        started.append(copy)
        copy.start()
        return copy

    scale = jnp.broadcast_to(scale_ref[...].astype(f32), (128, 128)).T
    gathered[row] = (scale * features_ref[...].astype(f32)).astype(bf16)
    pl.semaphore_wait(barrier, len(everyone))

    def gather(buffer, index, place, count, partner, up, down, arrived, hook):
        half = count // 2
        mine = buffer.at[index(0, place)]
        swap = send(mine, mine, partner)
        arrived(index(0, place))
        copies = {}
        for hop in range(1, half + 2):
            for piece in (0, 1):
                if hop == 1 and piece == 1:
                    swap.wait_recv()
                    arrived(index(1, place))
                for way in (UP, DOWN):
                    back_by = (place - (hop - 1)) % count if way == UP else (place + (hop - 1)) % count
                    if (way, hop - 1, piece) in copies:
                        copies[way, hop - 1, piece].wait_recv()
                        arrived(index(piece, back_by))
                    if hop < half or (hop == half and (way == UP) == (piece == 0)):
                        block = buffer.at[index(piece, back_by)]
                        copies[way, hop, piece] = send(block, block, up if way == UP else down)
            hook(hop)

    def reduce(own, place, count, partner, up, down, outs, ins, edge_send, edge_recv, ready, hook):
        half = count // 2
        copies = {}

        def value(way, piece, distance, dest, slot):
            total = own(piece, dest, slot)
            if (way, piece, distance + 1) in copies:
                copies[way, piece, distance + 1][0].wait_recv()
                total = total + ins[copies[way, piece, distance + 1][1]].astype(f32)
            return total

        number = 0
        for distance in range(half, 0, -1):
            ready(distance)
            for piece in (0, 1):
                for way in (UP, DOWN):
                    if distance == half and (way == UP) != (piece == 0):
                        continue
                    dest = (place + distance) % count if way == UP else (place - distance) % count
                    outs[number] = value(way, piece, distance, dest, number).astype(bf16)
                    copies[way, piece, distance] = (
                        send(outs.at[number], ins.at[number], up if way == UP else down), number
                    )
                    number += 1
            hook(distance)
        ready(0)

        def arrived_sum(piece):
            total = own(piece, place, number + piece)
            for way in (UP, DOWN):
                if (way, piece, 1) in copies:
                    copies[way, piece, 1][0].wait_recv()
                    total = total + ins[copies[way, piece, 1][1]].astype(f32)
            return total

        edge_send[...] = arrived_sum(1).astype(bf16)
        edge = send(edge_send, edge_recv, partner)
        mine = arrived_sum(0)
        hook(0)
        edge.wait_recv()
        return mine + edge_recv[...].astype(f32)

    def no_hook(step):
        return None

    def row_index(piece, y_at):
        return row_of(xl if piece == 0 else 1 - xl, y_at)

    def prepare(step):
        if step != 1:
            return

        def body(slot, carry):
            block = masks_ref[slot].astype(f32)
            masks[slot] = block.astype(bf16)
            masks_t[slot] = block.T.astype(bf16)
            return carry

        lax.fori_loop(0, slots, body, 0)
        products[slots] = jnp.zeros((128, 128), f32)
        back[slots] = jnp.zeros((128, 128), f32)

    gather(gathered, row_index, y, ny, lo_partner, y_peers[0], y_peers[ny - 2], no_hook, prepare)

    for slot in range(slots):
        products[slot] = jnp.dot(
            masks[slot], gathered[table[slot]], preferred_element_type=f32
        )

    def term(piece, z_at, core_at):
        x_hi = xh if piece == 0 else 1 - xh
        return products[table[4 * slots + col_of(x_hi, z_at, core_at)]]

    half_z = nz // 2
    pair_copies = {}
    number = 0
    for distance in range(half_z, -1, -1):
        first = number
        for piece in (0, 1):
            for way in (UP, DOWN):
                if distance in (half_z, 0) and (way == UP) != (piece == 0):
                    continue
                dest = (z + distance) % nz if way == UP else (z - distance) % nz
                pair_out[number] = term(piece, dest, 1 - core).astype(bf16)
                number += 1
        span = pl.ds(first, number - first)
        pair_copies[distance] = send(pair_out.at[span], pair_in.at[span], sibling)

    def own_forward(piece, dest, slot):
        return term(piece, dest, core) + pair_in[slot].astype(f32)

    summed = reduce(
        own_forward, z, nz, hi_partner, z_peers[0], z_peers[nz - 2], ring_out, ring_in,
        edge_out, edge_in, lambda distance: pair_copies[distance].wait_recv(), no_hook,
    )

    aggregated = (scale * summed).astype(bf16)
    weight = weight_ref[...]
    preact = jnp.dot(aggregated, weight, preferred_element_type=f32) + bias_ref[...]
    root = math.sqrt(2.0 / math.pi)
    square = preact * preact
    slope = jnp.tanh(root * (preact + 0.044715 * (square * preact)))
    cdf = 0.5 * (1.0 + slope)
    derivative = cdf + preact * (0.5 * (1.0 - slope * slope) * (root * (1.0 + 0.134145 * square)))
    grad_pre = (cotangent_ref[...].astype(f32) * derivative).astype(bf16)
    message = scale * lax.dot_general(
        grad_pre, weight, (((1,), (1,)), ((), ())), preferred_element_type=f32
    )

    def column_index(piece, z_at):
        return (core * 2 + (xh if piece == 0 else 1 - xh)) * nz + z_at

    messages[column_index(0, z)] = message.astype(bf16)

    chunk = parts.shape[2]
    state = {}

    def weight_start():
        hidden_ref[...] = (preact * cdf).astype(bf16)
        weight_part = lax.dot_general(
            aggregated, grad_pre, (((0,), (0,)), ((), ())), preferred_element_type=f32
        )
        bias_part = jnp.sum(grad_pre.astype(f32), axis=0, keepdims=True)
        lines = lax.broadcasted_iota(jnp.int32, (chunk, 128), 0)
        bias_tile = jnp.where(
            lines == 0, bias_part[:, :128], jnp.where(lines == 1, bias_part[:, 128:], 0.0)
        )
        for core_at in (0, 1):
            for y_at in range(ny):
                first = (core_at * ny + y_at) * chunk
                parts[core_at, y_at, :, :256] = weight_part[first : first + chunk]
                parts[core_at, y_at, :, 256:] = bias_tile
        state["pair"] = send(parts.at[1 - core], parts_in, sibling)

    def weight_y():
        state["pair"].wait_recv()
        halves[...] = parts[core] + parts_in[...]
        state["y"] = [
            send(halves.at[(y + j) % ny], y_in.at[j - 1], y_peers[j - 1]) for j in range(1, ny)
        ]

    def weight_x():
        total = halves[y]
        for j, copy in enumerate(state["y"]):
            copy.wait_recv()
            total = total + y_in[j]
        x_at = xh * 2 + xl
        x_terms[x_at] = total
        state["x"] = [
            send(x_terms.at[x_at], x_terms.at[x_at], peer)
            for peer in (lo_partner, hi_partner, far_partner)
        ]

    def weight_z():
        for copy in state["x"]:
            copy.wait_recv()
        z_terms[z] = (x_terms[0] + x_terms[1]) + (x_terms[2] + x_terms[3])
        state["z"] = [send(z_terms.at[z], z_terms.at[z], peer) for peer in z_peers]

    def weight_spread():
        for copy in state["z"]:
            copy.wait_recv()
        total = z_terms[0]
        for j in range(1, nz):
            total = total + z_terms[j]
        finals[core, y] = total
        state["spread"] = [
            send(finals.at[core, y], finals.at[core, y], peer) for peer in y_peers
        ]

    def weight_pair():
        for copy in state["spread"]:
            copy.wait_recv()
        state["last"] = send(finals.at[core], finals.at[core], sibling)

    def weight_store():
        state["last"].wait_recv()
        for core_at in (0, 1):
            for y_at in range(ny):
                first = (core_at * ny + y_at) * chunk
                grad_weight_ref[first : first + chunk, :] = finals[core_at, y_at, :, :256]
        grad_bias_ref[...] = finals[0, 0, 0:2, 256:]

    shared = []

    def share(index):
        shared.append(send(messages.at[index], messages.at[index], sibling))

    gather_steps = {1: weight_start, 3: weight_y, 5: weight_x, half_z + 1: weight_z}

    def gather_hook(step):
        if step in gather_steps:
            gather_steps[step]()

    gather(messages, column_index, z, nz, hi_partner, z_peers[0], z_peers[nz - 2], share, gather_hook)
    for copy in shared:
        copy.wait_recv()

    for slot in range(slots):
        product = jnp.dot(
            masks_t[slot], messages[table[slots + slot]], preferred_element_type=f32
        )
        back[slot] = product + back[table[2 * slots + slot]]

    def own_backward(piece, dest, slot):
        return back[table[3 * slots + row_index(piece, dest)]]

    reduce_steps = {2: weight_spread, 0: weight_pair}

    def reduce_hook(step):
        if step in reduce_steps:
            reduce_steps[step]()

    summed_back = reduce(
        own_backward, y, ny, lo_partner, y_peers[0], y_peers[ny - 2], back_out, back_in,
        back_edge_out, back_edge_in, no_hook, reduce_hook,
    )
    grad_features_ref[...] = (scale * summed_back).astype(bf16)
    weight_store()
    for copy in started:
        copy.wait_send()


def copies_of(ny, nz):
    def one_way(count):
        return 2 * (count - 1)

    gathers = (1 + one_way(ny)) + (1 + one_way(nz) + 2 * nz)
    reduces = (nz // 2 + 1) + (one_way(nz) + 1) + (one_way(ny) + 1)
    weights = 1 + (ny - 1) + 3 + (nz - 1) + (ny - 1) + 1
    return gathers + reduces + weights


def on_device(features, node_scale, weight, bias, block_rows, block_cols, block_masks, out_grad):
    ny, nz = lax.axis_size("row") // 2, lax.axis_size("col") // 4
    slots = block_masks.shape[2]
    row_ids, col_ids = block_rows.reshape(slots), block_cols.reshape(slots)
    numbers = jnp.arange(slots, dtype=jnp.int32)

    def named(match):
        found = jnp.max(jnp.where(match, numbers[None, :], -1), axis=1)
        return jnp.where(found < 0, slots, found)

    message_ids = (row_ids % 2) * (2 * nz) + (row_ids // (2 * nz)) * nz + (row_ids % (2 * nz)) // 2
    earlier = named((col_ids[:, None] == col_ids[None, :]) & (numbers[None, :] < numbers[:, None]))
    last = named(jnp.arange(2 * ny, dtype=jnp.int32)[:, None] == col_ids[None, :])
    owners = named(jnp.arange(4 * nz, dtype=jnp.int32)[:, None] == row_ids[None, :])
    pad = jnp.zeros((slots - 2 * ny,), jnp.int32)
    table = jnp.concatenate([col_ids, message_ids, earlier, last, pad, owners])

    bf16, f32 = jnp.bfloat16, jnp.float32
    chunk = weight.shape[0] // (2 * ny)
    block = (128, 128)
    vmem = pl.BlockSpec(memory_space=pltpu.VMEM)
    copies = copies_of(ny, nz)
    hidden, grad_features, grad_weight, grad_bias = pl.pallas_call(
        functools.partial(kernel, ny, nz),
        out_shape=(
            jax.ShapeDtypeStruct((128, 256), bf16),
            jax.ShapeDtypeStruct(block, bf16),
            jax.ShapeDtypeStruct((128, 256), f32),
            jax.ShapeDtypeStruct((2, 128), f32),
        ),
        in_specs=[pl.BlockSpec(memory_space=pltpu.SMEM)] + [vmem] * 6,
        out_specs=(vmem,) * 4,
        scratch_shapes=[
            pltpu.VMEM((slots,) + block, bf16),
            pltpu.VMEM((slots,) + block, bf16),
            pltpu.VMEM((2 * ny,) + block, bf16),
            pltpu.VMEM((slots + 1,) + block, f32),
            pltpu.VMEM((2 * nz,) + block, bf16),
            pltpu.VMEM((2 * nz,) + block, bf16),
            pltpu.VMEM((2 * nz - 2,) + block, bf16),
            pltpu.VMEM((2 * nz - 2,) + block, bf16),
            pltpu.VMEM(block, bf16),
            pltpu.VMEM(block, bf16),
            pltpu.VMEM((4 * nz,) + block, bf16),
            pltpu.VMEM((slots + 1,) + block, f32),
            pltpu.VMEM((2 * ny - 2,) + block, bf16),
            pltpu.VMEM((2 * ny - 2,) + block, bf16),
            pltpu.VMEM(block, bf16),
            pltpu.VMEM(block, bf16),
            pltpu.VMEM((2, ny, chunk, 384), f32),
            pltpu.VMEM((ny, chunk, 384), f32),
            pltpu.VMEM((ny, chunk, 384), f32),
            pltpu.VMEM((ny - 1, chunk, 384), f32),
            pltpu.VMEM((4, chunk, 384), f32),
            pltpu.VMEM((nz, chunk, 384), f32),
            pltpu.VMEM((2, ny, chunk, 384), f32),
            pltpu.SemaphoreType.DMA((copies,)),
            pltpu.SemaphoreType.DMA((copies,)),
        ],
        compiler_params=pltpu.CompilerParams(
            collective_id=0, has_side_effects=True, vmem_limit_bytes=40 * 1024 * 1024
        ),
        cost_estimate=pl.CostEstimate(
            flops=200_000_000, bytes_accessed=2_000_000, transcendentals=32768
        ),
    )(
        table, node_scale.reshape(1, 128), features, weight, bias.reshape(1, 256),
        block_masks.reshape(slots, 128, 128), out_grad,
    )
    return hidden, grad_features, grad_weight, grad_bias.reshape(256)


def solution(mesh):
    return jax.shard_map(
        on_device,
        mesh=mesh,
        in_specs=(
            P(("row", "col"), None),
            P(("row", "col")),
            P(),
            P(),
            P("row", "col", None),
            P("row", "col", None),
            P("row", "col", None, None, None),
            P(("row", "col"), None),
        ),
        out_specs=(P(("row", "col"), None), P(("row", "col"), None), P(), P()),
        check_vma=False,
    )
```

time: 934 us -> 113 us (0.12)
  waiting for transfers between devices: 695 us -> 0 us
  blocking collectives: 202 us -> 0 us
  Pallas kernels: 0 us -> 104 us
  between operations: 13.9 us -> 0.69 us
  matrix products: 9.9 us -> 0 us
    psum x1 -> x0, waiting for transfers between devices: 449 us -> none  [on_device(): grad_weight, grad_bias = lax.psum((weight_part, bias_part), ('row', 'col'))]
    reduce_scatter x2 -> x0, waiting for transfers between devices: 180 us -> none  [the longest x1 180 us: on_device(): lax.psum_scatter(partial_value, 'col', scatter_dimension=0, tiled=True)]
    psum x1 -> x0, blocking collectives: 107 us -> none  [on_device(): grad_weight, grad_bias = lax.psum((weight_part, bias_part), ('row', 'col'))]
    pallas_call x0 -> x1, Pallas kernels: none -> 104 us  [on_device(): pl.pallas_call(functools.partial(kernel, ny, nz), out_shape=(jax.ShapeDty...]
    all_gather x2 -> x0, blocking collectives: 95.4 us -> none  [the longest x1 64.8 us: on_device(): lax.all_gather(node_scale, 'col', axis=0, tiled=True)]
    all_gather x1 -> x0, waiting for transfers between devices: 65.8 us -> none  [on_device(): lax.all_gather(grad_pre, 'col', axis=0, tiled=True)]
    dot_general x7 -> x0, matrix products: 9.9 us -> none  [the longest x1 2.96 us: on_device(): jnp.dot(grads_all, weight.T, preferred_element_type=jnp.float32)]
  transfers between devices with their start and end apart: 4 -> 0, of which waited for: 3 -> 0; matrix products, arithmetic and copies ran while one was open for 0% -> 0% of each run, Pallas kernels for 0% -> 0%
where the time goes in v1:
time: 113 us
  Pallas kernels  104 us (92%)
  local copies, waits for them, and re-layouts  8.06 us (7%)
    pallas_call x1, Pallas kernels, on_device(): pl.pallas_call(functools.partial(kernel, ny, nz), out_shape=(jax.ShapeDty...  104 us
    unnamed x20, local copies, waits for them, and re-layouts  7.98 us

profile of v1, /device:TPU:1, one launch (start us, length us, event | category | flops | bytes accessed | tf_op | source)
XLA Modules:
  0.0 112.9 jit_solution(17409776071072831420)
XLA Ops:
  0.6 0.0 copy-start.7
  0.6 0.6 copy-done.7
  1.3 0.1 select_reduce_fusion
  1.4 0.0 copy-start.6
  1.4 0.6 copy-done.6
  2.0 0.2 select_reduce_fusion.1
  2.2 0.0 copy-start.4
  2.2 0.0 copy-start.5
  2.3 0.1 concatenate.3.table
  2.3 0.6 copy-done.4
  2.9 0.0 copy-done.5
  2.9 0.0 copy-start
  2.9 1.2 %copy-done = s32[1,1,16,128,128]{4,3,2,1,0:T(8,128)S(1)} copy-done((s32[1,1,16,128,128]{4,3,2,1,0:T(8,128)S(1)}, s32[1,1,16,128,128]{4,3,2,1,0:T(8,128)}, u32[]{:S(2)}) %copy-start) | copy-done | bytes 1048600
  4.1 0.0 copy-start.1
  4.1 0.8 copy-done.1
  5.0 0.0 copy-start.2
  5.0 0.8 copy-done.2
  5.8 0.0 copy-start.3
  5.8 0.8 copy-done.3
  6.6 103.9 %shard_map.111 = (bf16[128,256]{1,0:T(8,128)(2,1)S(1)}, bf16[128,128]{1,0:T(8,128)(2,1)S(1)}, f32[128,256]{1,0:T(8,128)S(1)}, f32[2,128]{1,0:T(2,128)S(1)}) custom-call(s32[112]{0:T(128)S(1)} %concatenate.3.table, bf16[1,128]{1,0:T(2,128)(2,1)S(1)} %bitcast.10, bf16[128,128]{1,0:T(8,128)(2,1)S(1)} %copy-done.3, bf16[128,256]{1,0:T(8,128)(2,1)S(1)} %copy-done.1, ...), custom_call_target="tpu_custom_call" | custom-call | flops 200000000 | bytes 2000000 | tf_op jit(solution)/shard_map/pallas_call | solution.py:340
  110.5 0.6 copy.16
  111.1 0.6 copy.17
  111.7 0.7 copy.18
  112.4 0.6 copy.19
  (3 shorter events, 0.0 us)
Async XLA Ops:
  0.6 0.7 copy-start.7
  1.4 0.7 copy-start.6
  2.2 0.7 copy-start.4
  2.2 0.7 copy-start.5
  2.9 1.2 %copy-start = (s32[1,1,16,128,128]{4,3,2,1,0:T(8,128)S(1)}, s32[1,1,16,128,128]{4,3,2,1,0:T(8,128)}, u32[]{:S(2)}) copy-start(s32[1,1,16,128,128]{4,3,2,1,0:T(8,128)} %param.14) | copy-start | bytes 3145732
  4.1 0.8 copy-start.1
  5.0 0.8 copy-start.2
  5.8 0.8 copy-start.3

commit v2 on v0

v2 whole, which is shorter than its diff:
```python
import functools
import math

import jax
import jax.numpy as jnp
from jax import lax
from jax.experimental import pallas as pl
from jax.experimental.pallas import tpu as pltpu
from jax.sharding import PartitionSpec as P

MESH = pl.DeviceIdType.MESH


def far_first(count):
    return sorted(range(1, count), key=lambda step: -min(step, count - step))


def kernel(
    ny, nz,
    features_hbm, scale_hbm, weight_hbm, bias_hbm, rows_hbm, cols_hbm, masks_hbm, cotangent_hbm,
    hidden_ref, grad_features_ref, grad_weight_ref, grad_bias_ref,
    features_ref, scale_ref, weight_ref, bias_ref, row_ids, col_ids, masks_ref, cotangent_ref,
    message_ids, earlier, last, owners,
    masks, masks_t, gathered, products, pair_out, pair_in, edge_out, edge_in, ring_out, ring_in,
    messages, back, back_edge_out, back_edge_in, back_out, back_in,
    parts, parts_in, halves, y_in, x_terms, z_terms, finals,
    load_sems, send_sems, recv_sems,
):
    f32, bf16 = jnp.float32, jnp.bfloat16
    slots = masks.shape[0]
    row, col = lax.axis_index("row"), lax.axis_index("col")
    xl, y = row // ny, row % ny
    xh, z, core = col // (2 * nz), (col % (2 * nz)) // 2, col % 2

    def row_of(x_lo, y_at):
        return x_lo * ny + y_at

    def col_of(x_hi, z_at, core_at):
        return x_hi * (2 * nz) + z_at * 2 + core_at

    sibling = (row, col_of(xh, z, 1 - core))
    lo_partner = (row_of(1 - xl, y), col)
    hi_partner = (row, col_of(1 - xh, z, core))
    far_partner = (row_of(1 - xl, y), col_of(1 - xh, z, core))
    y_far, z_far = far_first(ny), far_first(nz)
    y_peer = {j: (row_of(xl, (y + j) % ny), col) for j in y_far}
    z_peer = {j: (row, col_of(xh, (z + j) % nz, core)) for j in z_far}

    barrier = pltpu.get_barrier_semaphore()
    everyone = [sibling, lo_partner, hi_partner, far_partner]
    everyone = [y_peer[j] for j in y_far] + everyone + [z_peer[j] for j in z_far]
    for peer in everyone:
        pl.semaphore_signal(barrier, inc=1, device_id=peer, device_id_type=MESH)

    loads = []
    for number, (src, dst) in enumerate((
        (features_hbm, features_ref), (scale_hbm, scale_ref), (rows_hbm, row_ids),
        (cols_hbm, col_ids), (masks_hbm, masks_ref), (weight_hbm, weight_ref),
        (bias_hbm, bias_ref), (cotangent_hbm, cotangent_ref),
    )):
        load = pltpu.make_async_copy(src, dst, load_sems.at[number])
        load.start()
        loads.append(load)

    started = []

    def send(src, dst, peer):
        number = len(started)
        copy = pltpu.make_async_remote_copy(
            src_ref=src, dst_ref=dst, send_sem=send_sems.at[number], recv_sem=recv_sems.at[number],
            device_id=peer, device_id_type=MESH,
        )
        started.append(copy)
        copy.start()
        return copy

    loads[0].wait()
    loads[1].wait()
    scale = jnp.broadcast_to(scale_ref[...].astype(f32), (128, 128)).T
    gathered[row] = (scale * features_ref[...].astype(f32)).astype(bf16)
    pl.semaphore_wait(barrier, len(everyone))

    own = gathered.at[row]
    direct = {j: send(own, own, y_peer[j]) for j in y_far}
    swapped = [send(own, own, lo_partner)]

    for load in loads[2:5]:
        load.wait()
    def find_owner(place, carry):
        found = slots
        for slot in range(slots):
            found = jnp.where(row_ids[0, 0, slot] == place, slot, found)
        owners[place] = found
        return carry

    def prepare(slot, carry):
        masks[slot] = masks_ref[0, 0, slot].astype(f32).astype(bf16)
        return carry

    lax.fori_loop(0, slots, prepare, 0)
    products[slots] = jnp.zeros((128, 128), f32)

    for j in y_far:
        direct[j].wait_recv()
        block = gathered.at[row_of(xl, (y - j) % ny)]
        swapped.append(send(block, block, lo_partner))
    lax.fori_loop(0, 4 * nz, find_owner, 0)
    for copy in swapped:
        copy.wait_recv()

    for slot in range(slots):
        products[slot] = jnp.dot(
            masks[slot], gathered[col_ids[0, 0, slot]], preferred_element_type=f32
        )

    def term(x_hi, j, core_at):
        return products[owners[col_of(x_hi, (z + j) % nz, core_at)]]

    z_order = z_far + [0]
    group = 3
    pair_copies = {}
    for piece, x_hi in enumerate((1 - xh, xh)):
        for place, j in enumerate(z_order):
            pair_out[piece, place] = term(x_hi, j, 1 - core).astype(bf16)
            if place % group == group - 1:
                span = pl.ds(place - group + 1, group)
                pair_copies[piece, place // group] = send(
                    pair_out.at[piece, span], pair_in.at[piece, span], sibling
                )
    edges = {}
    for place, j in enumerate(z_order):
        if place % group == 0:
            pair_copies[0, place // group].wait_recv()
        total = term(1 - xh, j, core) + pair_in[0, place].astype(f32)
        edge_out[place] = total.astype(bf16)
        edges[j] = send(edge_out.at[place], edge_in.at[place], hi_partner)
    direct = {}
    summed = None
    for place, j in enumerate(z_order):
        if place % group == 0:
            pair_copies[1, place // group].wait_recv()
        total = term(xh, j, core) + pair_in[1, place].astype(f32)
        edges[j].wait_recv()
        total = total + edge_in[place].astype(f32)
        if j == 0:
            summed = total
        else:
            ring_out[j - 1] = total.astype(bf16)
            direct[j] = send(ring_out.at[j - 1], ring_in.at[j - 1], z_peer[j])
    for slot in range(slots):
        row_id = row_ids[0, 0, slot]
        message_ids[slot] = (
            (row_id % 2) * (2 * nz) + (row_id // (2 * nz)) * nz + (row_id % (2 * nz)) // 2
        )
        found = slots
        for other in range(slot):
            found = jnp.where(col_ids[0, 0, other] == col_ids[0, 0, slot], other, found)
        earlier[slot] = found

    def find_last(place, carry):
        found = slots
        for slot in range(slots):
            found = jnp.where(col_ids[0, 0, slot] == place, slot, found)
        last[place] = found
        return carry

    def transpose(slot, carry):
        masks_t[slot] = masks_ref[0, 0, slot].astype(f32).T.astype(bf16)
        return carry

    lax.fori_loop(0, 2 * ny, find_last, 0)
    lax.fori_loop(0, slots, transpose, 0)
    back[slots] = jnp.zeros((128, 128), f32)
    for load in loads[5:]:
        load.wait()
    for j in z_far:
        direct[j].wait_recv()
        summed = summed + ring_in[j - 1].astype(f32)

    aggregated = (scale * summed).astype(bf16)
    weight = weight_ref[...]
    preact = jnp.dot(aggregated, weight, preferred_element_type=f32) + bias_ref[...]
    root = math.sqrt(2.0 / math.pi)
    square = preact * preact
    slope = jnp.tanh(root * (preact + 0.044715 * (square * preact)))
    cdf = 0.5 * (1.0 + slope)
    derivative = cdf + preact * (0.5 * (1.0 - slope * slope) * (root * (1.0 + 0.134145 * square)))
    grad_pre = (cotangent_ref[...].astype(f32) * derivative).astype(bf16)
    message = scale * lax.dot_general(
        grad_pre, weight, (((1,), (1,)), ((), ())), preferred_element_type=f32
    )

    shared = []

    def message_at(x_hi, z_at):
        return messages.at[(core * 2 + x_hi) * nz + z_at]

    def share(block):
        shared.append(send(block, block, sibling))

    messages[(core * 2 + xh) * nz + z] = message.astype(bf16)
    own = message_at(xh, z)
    direct = {j: send(own, own, z_peer[j]) for j in z_far}
    swapped = [send(own, own, hi_partner)]
    share(own)

    chunk = parts.shape[2]

    hidden_ref[...] = (preact * cdf).astype(bf16)
    weight_part = lax.dot_general(
        aggregated, grad_pre, (((0,), (0,)), ((), ())), preferred_element_type=f32
    )
    bias_part = jnp.sum(grad_pre.astype(f32), axis=0, keepdims=True)
    lines = lax.broadcasted_iota(jnp.int32, (chunk, 128), 0)
    bias_tile = jnp.where(
        lines == 0, bias_part[:, :128], jnp.where(lines == 1, bias_part[:, 128:], 0.0)
    )
    for core_at in (0, 1):
        for y_at in range(ny):
            first = (core_at * ny + y_at) * chunk
            parts[core_at, y_at, :, :256] = weight_part[first : first + chunk]
            parts[core_at, y_at, :, 256:] = bias_tile
    pair = send(parts.at[1 - core], parts_in, sibling)
    pair.wait_recv()
    halves[...] = parts[core] + parts_in[...]
    y_copies = {j: send(halves.at[(y + j) % ny], y_in.at[j - 1], y_peer[j]) for j in y_far}

    for number, j in enumerate(z_far):
        direct[j].wait_recv()
        block = message_at(xh, (z - j) % nz)
        swapped.append(send(block, block, hi_partner))
        share(block)
        if number == nz // 2:
            total = halves[y]
            for j in y_far:
                y_copies[j].wait_recv()
                total = total + y_in[j - 1]
            x_at = xh * 2 + xl
            x_terms[x_at] = total
            x_copies = [
                send(x_terms.at[x_at], x_terms.at[x_at], peer)
                for peer in (lo_partner, hi_partner, far_partner)
            ]

    for copy in x_copies:
        copy.wait_recv()
    z_terms[z] = (x_terms[0] + x_terms[1]) + (x_terms[2] + x_terms[3])
    z_copies = [send(z_terms.at[z], z_terms.at[z], z_peer[j]) for j in z_far]


    for place, copy in enumerate(swapped):
        copy.wait_recv()
        share(message_at(1 - xh, z if place == 0 else (z - z_far[place - 1]) % nz))

    for copy in shared:
        copy.wait_recv()

    for slot in range(slots):
        product = jnp.dot(
            masks_t[slot], messages[message_ids[slot]], preferred_element_type=f32
        )
        back[slot] = product + back[earlier[slot]]

    def back_term(x_lo, j):
        return back[last[row_of(x_lo, (y + j) % ny)]]

    y_order = y_far + [0]
    edges = {}
    for place, j in enumerate(y_order):
        back_edge_out[place] = back_term(1 - xl, j).astype(bf16)
        edges[j] = send(back_edge_out.at[place], back_edge_in.at[place], lo_partner)
    direct = {}
    summed = None
    for place, j in enumerate(y_order):
        total = back_term(xl, j)
        edges[j].wait_recv()
        total = total + back_edge_in[place].astype(f32)
        if j == 0:
            summed = total
        else:
            back_out[j - 1] = total.astype(bf16)
            direct[j] = send(back_out.at[j - 1], back_in.at[j - 1], y_peer[j])

    for copy in z_copies:
        copy.wait_recv()
    total = z_terms[0]
    for z_at in range(1, nz):
        total = total + z_terms[z_at]
    finals[core, y] = total
    own = finals.at[core, y]
    y_copies = [send(own, own, y_peer[j]) for j in y_far]

    for j in y_far:
        direct[j].wait_recv()
        summed = summed + back_in[j - 1].astype(f32)
    grad_features_ref[...] = (scale * summed).astype(bf16)

    for copy in y_copies:
        copy.wait_recv()
    pair = send(finals.at[core], finals.at[core], sibling)
    for copy in started[:-1]:
        copy.wait_send()
    pair.wait()
    for core_at in (0, 1):
        for y_at in range(ny):
            first = (core_at * ny + y_at) * chunk
            grad_weight_ref[first : first + chunk, :] = finals[core_at, y_at, :, :256]
    grad_bias_ref[...] = finals[0, 0, 0:2, 256:]


def store(*refs):
    for number in range(4):
        refs[4 + number][...] = refs[number][...]


def copies_of(ny, nz):
    forward = (2 * ny - 1) + 2 * (nz // 3) + nz + (nz - 1)
    backward = (2 * nz - 1) + 2 * nz + ny + (ny - 1)
    weights = 1 + (ny - 1) + 3 + (nz - 1) + (ny - 1) + 1
    return forward + backward + weights


def on_device(features, node_scale, weight, bias, block_rows, block_cols, block_masks, out_grad):
    ny, nz = lax.axis_size("row") // 2, lax.axis_size("col") // 4
    slots = block_masks.shape[2]
    bf16, f32, i32 = jnp.bfloat16, jnp.float32, jnp.int32
    chunk = weight.shape[0] // (2 * ny)
    block = (128, 128)
    anywhere = pl.BlockSpec(memory_space=pl.ANY)
    vmem = pl.BlockSpec(memory_space=pltpu.VMEM)
    copies = copies_of(ny, nz)
    results = (
        jax.ShapeDtypeStruct((128, 256), bf16),
        jax.ShapeDtypeStruct(block, bf16),
        jax.ShapeDtypeStruct((128, 256), f32),
        jax.ShapeDtypeStruct((2, 128), f32),
    )
    outs = pl.pallas_call(
        functools.partial(kernel, ny, nz),
        out_shape=results,
        in_specs=[anywhere] * 8,
        out_specs=(vmem,) * 4,
        scratch_shapes=[
            pltpu.VMEM(block, bf16),
            pltpu.VMEM((1, 128), bf16),
            pltpu.VMEM((128, 256), bf16),
            pltpu.VMEM((1, 256), f32),
            pltpu.SMEM((1, 1, slots), i32),
            pltpu.SMEM((1, 1, slots), i32),
            pltpu.VMEM((1, 1, slots) + block, i32),
            pltpu.VMEM((128, 256), bf16),
            pltpu.SMEM((slots,), i32),
            pltpu.SMEM((slots,), i32),
            pltpu.SMEM((2 * ny,), i32),
            pltpu.SMEM((4 * nz,), i32),
            pltpu.VMEM((slots,) + block, bf16),
            pltpu.VMEM((slots,) + block, bf16),
            pltpu.VMEM((2 * ny,) + block, bf16),
            pltpu.VMEM((slots + 1,) + block, f32),
            pltpu.VMEM((2, nz) + block, bf16),
            pltpu.VMEM((2, nz) + block, bf16),
            pltpu.VMEM((nz,) + block, bf16),
            pltpu.VMEM((nz,) + block, bf16),
            pltpu.VMEM((nz - 1,) + block, bf16),
            pltpu.VMEM((nz - 1,) + block, bf16),
            pltpu.VMEM((4 * nz,) + block, bf16),
            pltpu.VMEM((slots + 1,) + block, f32),
            pltpu.VMEM((ny,) + block, bf16),
            pltpu.VMEM((ny,) + block, bf16),
            pltpu.VMEM((ny - 1,) + block, bf16),
            pltpu.VMEM((ny - 1,) + block, bf16),
            pltpu.VMEM((2, ny, chunk, 384), f32),
            pltpu.VMEM((ny, chunk, 384), f32),
            pltpu.VMEM((ny, chunk, 384), f32),
            pltpu.VMEM((ny - 1, chunk, 384), f32),
            pltpu.VMEM((4, chunk, 384), f32),
            pltpu.VMEM((nz, chunk, 384), f32),
            pltpu.VMEM((2, ny, chunk, 384), f32),
            pltpu.SemaphoreType.DMA((8,)),
            pltpu.SemaphoreType.DMA((copies,)),
            pltpu.SemaphoreType.DMA((copies,)),
        ],
        compiler_params=pltpu.CompilerParams(
            collective_id=0, has_side_effects=True, vmem_limit_bytes=60 * 1024 * 1024
        ),
        cost_estimate=pl.CostEstimate(
            flops=200_000_000, bytes_accessed=2_000_000, transcendentals=32768
        ),
    )(
        features, node_scale.reshape(1, 128), weight, bias.reshape(1, 256),
        block_rows, block_cols, block_masks, out_grad,
    )
    hidden, grad_features, grad_weight, grad_bias = pl.pallas_call(
        store,
        out_shape=results,
        in_specs=[vmem] * 4,
        out_specs=(vmem,) * 4,
    )(*outs)
    return hidden, grad_features, grad_weight, grad_bias.reshape(256)


def solution(mesh):
    return jax.shard_map(
        on_device,
        mesh=mesh,
        in_specs=(
            P(("row", "col"), None),
            P(("row", "col")),
            P(),
            P(),
            P("row", "col", None),
            P("row", "col", None),
            P("row", "col", None, None, None),
            P(("row", "col"), None),
        ),
        out_specs=(P(("row", "col"), None), P(("row", "col"), None), P(), P()),
        check_vma=False,
    )
```

time: 934 us -> 93.8 us (0.10)
  waiting for transfers between devices: 695 us -> 0 us
  blocking collectives: 202 us -> 0 us
  Pallas kernels: 0 us -> 93 us
  between operations: 13.9 us -> 0.64 us
  matrix products: 9.9 us -> 0 us
    psum x1 -> x0, waiting for transfers between devices: 449 us -> none  [on_device(): grad_weight, grad_bias = lax.psum((weight_part, bias_part), ('row', 'col'))]
    reduce_scatter x2 -> x0, waiting for transfers between devices: 180 us -> none  [the longest x1 180 us: on_device(): lax.psum_scatter(partial_value, 'col', scatter_dimension=0, tiled=True)]
    psum x1 -> x0, blocking collectives: 107 us -> none  [on_device(): grad_weight, grad_bias = lax.psum((weight_part, bias_part), ('row', 'col'))]
    all_gather x2 -> x0, blocking collectives: 95.4 us -> none  [the longest x1 64.8 us: on_device(): lax.all_gather(node_scale, 'col', axis=0, tiled=True)]
    pallas_call x0 -> x2, Pallas kernels: none -> 93 us  [the longest x1 91.4 us: on_device(): pl.pallas_call(functools.partial(kernel, ny, nz), out_shape=results, in_s...]
    all_gather x1 -> x0, waiting for transfers between devices: 65.8 us -> none  [on_device(): lax.all_gather(grad_pre, 'col', axis=0, tiled=True)]
    dot_general x7 -> x0, matrix products: 9.9 us -> none  [the longest x1 2.96 us: on_device(): jnp.dot(grads_all, weight.T, preferred_element_type=jnp.float32)]
  transfers between devices with their start and end apart: 4 -> 0, of which waited for: 3 -> 0; matrix products, arithmetic and copies ran while one was open for 0% -> 0% of each run, Pallas kernels for 0% -> 0%
where the time goes in v2:
time: 93.8 us; the launch traced here: 93.7 us
  Pallas kernels  93 us (99%)
    pallas_call x1, Pallas kernels, on_device(): pl.pallas_call(functools.partial(kernel, ny, nz), out_shape=results, in_s...  91.4 us

profile of v2, /device:TPU:1, one launch (start us, length us, event | category | flops | bytes accessed | tf_op | source)
XLA Modules:
  0.0 93.7 jit_solution(12300453237567118887)
XLA Ops:
  0.6 91.4 %shard_map.111 = (bf16[128,256]{1,0:T(8,128)(2,1)}, bf16[128,128]{1,0:T(8,128)(2,1)}, f32[128,256]{1,0:T(8,128)}, f32[2,128]{1,0:T(2,128)}) custom-call(bf16[128,128]{1,0:T(8,128)(2,1)} %features_hbm.1, bf16[1,128]{1,0:T(2,128)(2,1)} %bitcast.4, bf16[128,256]{1,0:T(8,128)(2,1)} %weight_hbm.1, f32[1,256]{1,0:T(1,128)} %bitcast.3, s32[1,1,16]{2,1,0:T(1,128)} %rows_hbm.1, ...), custom_call_target="tpu_custom_call" | custom-call | flops 200000000 | bytes 2000000 | tf_op jit(solution)/shard_map/pallas_call | solution.py:338
  92.0 1.7 %shard_map.112 = (bf16[128,256]{1,0:T(8,128)(2,1)}, bf16[128,128]{1,0:T(8,128)(2,1)}, f32[128,256]{1,0:T(8,128)}, f32[2,128]{1,0:T(2,128)}) custom-call(bf16[128,256]{1,0:T(8,128)(2,1)} %get-tuple-element.12.refs_0_, bf16[128,128]{1,0:T(8,128)(2,1)} %get-tuple-element.13.refs_1_, f32[128,256]{1,0:T(8,128)} %get-tuple-element.14.refs_2_, ...), custom_call_target="tpu_custom_call" | custom-call | tf_op jit(solution)/shard_map/pallas_call | solution.py:393

commit v3 on v2

--- a/solution.py
+++ b/solution.py
@@ -134,19 +134,53 @@
         total = term(1 - xh, j, core) + pair_in[0, place].astype(f32)
         edge_out[place] = total.astype(bf16)
         edges[j] = send(edge_out.at[place], edge_in.at[place], hi_partner)
-    direct = {}
-    summed = None
-    for place, j in enumerate(z_order):
-        if place % group == 0:
+    reach = nz // 4
+    half = pl.ds(0, 64), pl.ds(64, 64)
+
+    def near_sum(j):
+        place = z_order.index(j)
+        if place // group not in taken:
+            taken.add(place // group)
             pair_copies[1, place // group].wait_recv()
         total = term(xh, j, core) + pair_in[1, place].astype(f32)
         edges[j].wait_recv()
-        total = total + edge_in[place].astype(f32)
-        if j == 0:
-            summed = total
+        return total + edge_in[place].astype(f32)
+
+    taken = set()
+    direct, relayed = {}, {}
+    far_steps = [j for j in z_far if reach < j < nz - reach]
+    near_steps = [j for j in z_far if j not in far_steps and j not in (reach, nz - reach)]
+    for j in far_steps:
+        ring_out[j - 1] = near_sum(j).astype(bf16)
+        if 2 * j == nz:
+            for way, hop in enumerate((reach, nz - reach)):
+                relayed[j, way] = send(
+                    ring_out.at[j - 1, half[way]], ring_in.at[j - 1, half[way]], z_peer[hop]
+                )
         else:
-            ring_out[j - 1] = total.astype(bf16)
-            direct[j] = send(ring_out.at[j - 1], ring_in.at[j - 1], z_peer[j])
+            hop = j - reach if 2 * j < nz else j + reach
+            relayed[j] = send(ring_out.at[j - 1], ring_in.at[j - 1], z_peer[hop])
+    relay_sums = {j: near_sum(j) for j in (reach, nz - reach)}
+    for j in near_steps:
+        ring_out[j - 1] = near_sum(j).astype(bf16)
+        direct[j] = send(ring_out.at[j - 1], ring_in.at[j - 1], z_peer[j])
+    summed = near_sum(0)
+    for way, j in enumerate((reach, nz - reach)):
+        total = relay_sums[j]
+        for far in far_steps:
+            if 2 * far != nz and (2 * far < nz) == (way == 0):
+                relayed[far].wait_recv()
+                total = total + ring_in[far - 1].astype(f32)
+        relayed[nz // 2, way].wait_recv()
+        middle = ring_in[nz // 2 - 1, 64 * way : 64 * way + 64, :].astype(f32)
+        if way == 0:
+            ring_out[j - 1, :64, :] = (total[:64] + middle).astype(bf16)
+            ring_out[j - 1, 64:, :] = total[64:].astype(bf16)
+        else:
+            ring_out[j - 1, :64, :] = total[:64].astype(bf16)
+            ring_out[j - 1, 64:, :] = (total[64:] + middle).astype(bf16)
+        direct[j] = send(ring_out.at[j - 1], ring_in.at[j - 1], z_peer[j])
+
     for slot in range(slots):
         row_id = row_ids[0, 0, slot]
         message_ids[slot] = (
@@ -173,7 +207,7 @@
     back[slots] = jnp.zeros((128, 128), f32)
     for load in loads[5:]:
         load.wait()
-    for j in z_far:
+    for j in near_steps + [reach, nz - reach]:
         direct[j].wait_recv()
         summed = summed + ring_in[j - 1].astype(f32)
 
@@ -200,8 +234,10 @@
 
     messages[(core * 2 + xh) * nz + z] = message.astype(bf16)
     own = message_at(xh, z)
-    direct = {j: send(own, own, z_peer[j]) for j in z_far}
-    swapped = [send(own, own, hi_partner)]
+    direct = {j: send(own, own, z_peer[j]) for j in (reach, nz - reach)}
+    swapped = {0: send(own, own, hi_partner)}
+    for j in near_steps:
+        direct[j] = send(own, own, z_peer[j])
     share(own)
 
     chunk = parts.shape[2]
@@ -221,36 +257,65 @@
             parts[core_at, y_at, :, :256] = weight_part[first : first + chunk]
             parts[core_at, y_at, :, 256:] = bias_tile
     pair = send(parts.at[1 - core], parts_in, sibling)
+    def pass_on(j):
+        block = message_at(xh, (z - j) % nz)
+        swapped[j] = send(block, block, hi_partner)
+        share(block)
+
+    relayed = {}
+    for way, j in enumerate((reach, nz - reach)):
+        direct[j].wait_recv()
+        place = (core * 2 + xh) * nz + (z - j) % nz
+        for hop in range(reach, 0, -1):
+            far = reach + hop if way == 0 else nz - reach - hop
+            peer = z_peer[hop if way == 0 else nz - hop]
+            if hop == reach:
+                part = messages.at[place, half[way]]
+                relayed[far, way] = send(part, part, peer)
+            else:
+                part = messages.at[place]
+                relayed[far] = send(part, part, peer)
+        pass_on(j)
+    for j in near_steps:
+        direct[j].wait_recv()
+        pass_on(j)
+
     pair.wait_recv()
     halves[...] = parts[core] + parts_in[...]
     y_copies = {j: send(halves.at[(y + j) % ny], y_in.at[j - 1], y_peer[j]) for j in y_far}
 
-    for number, j in enumerate(z_far):
-        direct[j].wait_recv()
-        block = message_at(xh, (z - j) % nz)
-        swapped.append(send(block, block, hi_partner))
-        share(block)
-        if number == nz // 2:
-            total = halves[y]
-            for j in y_far:
-                y_copies[j].wait_recv()
-                total = total + y_in[j - 1]
-            x_at = xh * 2 + xl
-            x_terms[x_at] = total
-            x_copies = [
-                send(x_terms.at[x_at], x_terms.at[x_at], peer)
-                for peer in (lo_partner, hi_partner, far_partner)
-            ]
+    for j in far_steps[::-1]:
+        if 2 * j == nz:
+            relayed[j, 0].wait_recv()
+            relayed[j, 1].wait_recv()
+        else:
+            relayed[j].wait_recv()
+        pass_on(j)
+
+    order = [0, reach, nz - reach] + near_steps
+    for j in order:
+        swapped[j].wait_recv()
+        share(message_at(1 - xh, (z - j) % nz))
+
+    total = halves[y]
+    for j in y_far:
+        y_copies[j].wait_recv()
+        total = total + y_in[j - 1]
+    x_at = xh * 2 + xl
+    x_terms[x_at] = total
+    x_copies = [
+        send(x_terms.at[x_at], x_terms.at[x_at], peer)
+        for peer in (lo_partner, hi_partner, far_partner)
+    ]
+
+    for j in far_steps[::-1]:
+        swapped[j].wait_recv()
+        share(message_at(1 - xh, (z - j) % nz))
 
     for copy in x_copies:
         copy.wait_recv()
     z_terms[z] = (x_terms[0] + x_terms[1]) + (x_terms[2] + x_terms[3])
     z_copies = [send(z_terms.at[z], z_terms.at[z], z_peer[j]) for j in z_far]
-
-
-    for place, copy in enumerate(swapped):
-        copy.wait_recv()
-        share(message_at(1 - xh, z if place == 0 else (z - z_far[place - 1]) % nz))
 
     for copy in shared:
         copy.wait_recv()
@@ -314,8 +379,8 @@
 
 
 def copies_of(ny, nz):
-    forward = (2 * ny - 1) + 2 * (nz // 3) + nz + (nz - 1)
-    backward = (2 * nz - 1) + 2 * nz + ny + (ny - 1)
+    forward = (2 * ny - 1) + 2 * (nz // 3) + nz + nz
+    backward = nz + nz + 2 * nz + ny + (ny - 1)
     weights = 1 + (ny - 1) + 3 + (nz - 1) + (ny - 1) + 1
     return forward + backward + weights
 

time: 93.8 us -> 86.1 us (0.918)
  Pallas kernels: 93 us -> 85.3 us
    pallas_call x1, Pallas kernels: 91.4 us -> 83.7 us  [on_device(): pl.pallas_call(functools.partial(kernel, ny, nz), out_shape=results, in_s...]
where the time goes in v3:
time: 86.1 us; the launch traced here: 86 us
  Pallas kernels  85.3 us (99%)
    pallas_call x1, Pallas kernels, on_device(): pl.pallas_call(functools.partial(kernel, ny, nz), out_shape=results, in_s...  83.7 us

profile of v3, /device:TPU:1, one launch (start us, length us, event | category | flops | bytes accessed | tf_op | source)
XLA Modules:
  0.0 86.0 jit_solution(8305935616899527012)
XLA Ops:
  0.6 83.7 %shard_map.111 = (bf16[128,256]{1,0:T(8,128)(2,1)}, bf16[128,128]{1,0:T(8,128)(2,1)}, f32[128,256]{1,0:T(8,128)}, f32[2,128]{1,0:T(2,128)}) custom-call(bf16[128,128]{1,0:T(8,128)(2,1)} %features_hbm.1, bf16[1,128]{1,0:T(2,128)(2,1)} %bitcast.4, bf16[128,256]{1,0:T(8,128)(2,1)} %weight_hbm.1, f32[1,256]{1,0:T(1,128)} %bitcast.3, s32[1,1,16]{2,1,0:T(1,128)} %rows_hbm.1, ...), custom_call_target="tpu_custom_call" | custom-call | flops 200000000 | bytes 2000000 | tf_op jit(solution)/shard_map/pallas_call | solution.py:403
  84.3 1.7 %shard_map.112 = (bf16[128,256]{1,0:T(8,128)(2,1)}, bf16[128,128]{1,0:T(8,128)(2,1)}, f32[128,256]{1,0:T(8,128)}, f32[2,128]{1,0:T(2,128)}) custom-call(bf16[128,256]{1,0:T(8,128)(2,1)} %get-tuple-element.12.refs_0_, bf16[128,128]{1,0:T(8,128)(2,1)} %get-tuple-element.13.refs_1_, f32[128,256]{1,0:T(8,128)} %get-tuple-element.14.refs_2_, ...), custom_call_target="tpu_custom_call" | custom-call | tf_op jit(solution)/shard_map/pallas_call | solution.py:458

commit v4 on v3

--- a/solution.py
+++ b/solution.py
@@ -21,8 +21,8 @@
     hidden_ref, grad_features_ref, grad_weight_ref, grad_bias_ref,
     features_ref, scale_ref, weight_ref, bias_ref, row_ids, col_ids, masks_ref, cotangent_ref,
     message_ids, earlier, last, owners,
-    masks, masks_t, gathered, products, pair_out, pair_in, edge_out, edge_in, ring_out, ring_in,
-    messages, back, back_edge_out, back_edge_in, back_out, back_in,
+    masks, masks_t, gathered, products, pair_out, pair_in, near_out, near_in, edge_out, edge_in, ring_out, ring_in,
+    messages, back, beside_out, beside_in, back_edge_out, back_edge_in, back_out, back_in,
     parts, parts_in, halves, y_in, x_terms, z_terms, finals,
     load_sems, send_sems, recv_sems,
 ):
@@ -44,11 +44,17 @@
     far_partner = (row_of(1 - xl, y), col_of(1 - xh, z, core))
     y_far, z_far = far_first(ny), far_first(nz)
     y_peer = {j: (row_of(xl, (y + j) % ny), col) for j in y_far}
-    z_peer = {j: (row, col_of(xh, (z + j) % nz, core)) for j in z_far}
+    reach = nz // 4
+    ends = (reach, nz - reach)
+    far_steps = [j for j in z_far if reach < j < nz - reach]
+    near_steps = [j for j in z_far if j not in far_steps and j not in ends]
+    z_peer = {
+        j: (row, col_of(xh, (z + j) % nz, core)) for j in list(ends) + near_steps
+    }
 
     barrier = pltpu.get_barrier_semaphore()
     everyone = [sibling, lo_partner, hi_partner, far_partner]
-    everyone = [y_peer[j] for j in y_far] + everyone + [z_peer[j] for j in z_far]
+    everyone = [y_peer[j] for j in y_far] + list(z_peer.values()) + everyone
     for peer in everyone:
         pl.semaphore_signal(barrier, inc=1, device_id=peer, device_id_type=MESH)
 
@@ -74,6 +80,13 @@
         copy.start()
         return copy
 
+    drained = []
+
+    def drain(count):
+        for copy in started[len(drained) : count]:
+            copy.wait_send()
+            drained.append(copy)
+
     loads[0].wait()
     loads[1].wait()
     scale = jnp.broadcast_to(scale_ref[...].astype(f32), (128, 128)).T
@@ -98,14 +111,18 @@
         return carry
 
     lax.fori_loop(0, slots, prepare, 0)
+    swapped[0].wait_recv()
+    other = gathered.at[row_of(1 - xl, y)]
+    crossed = [send(other, other, y_peer[j]) for j in (1, ny - 1)]
     products[slots] = jnp.zeros((128, 128), f32)
 
     for j in y_far:
         direct[j].wait_recv()
-        block = gathered.at[row_of(xl, (y - j) % ny)]
-        swapped.append(send(block, block, lo_partner))
+        if j not in (1, ny - 1):
+            block = gathered.at[row_of(xl, (y - j) % ny)]
+            swapped.append(send(block, block, lo_partner))
     lax.fori_loop(0, 4 * nz, find_owner, 0)
-    for copy in swapped:
+    for copy in swapped[1:] + crossed:
         copy.wait_recv()
 
     for slot in range(slots):
@@ -127,45 +144,51 @@
                 pair_copies[piece, place // group] = send(
                     pair_out.at[piece, span], pair_in.at[piece, span], sibling
                 )
+    taken = set()
+
+    def pair_sum(piece, j):
+        place = z_order.index(j)
+        if (piece, place // group) not in taken:
+            taken.add((piece, place // group))
+            pair_copies[piece, place // group].wait_recv()
+        x_hi = 1 - xh if piece == 0 else xh
+        return term(x_hi, j, core) + pair_in[piece, place].astype(f32)
+
     edges = {}
-    for place, j in enumerate(z_order):
-        if place % group == 0:
-            pair_copies[0, place // group].wait_recv()
-        total = term(1 - xh, j, core) + pair_in[0, place].astype(f32)
-        edge_out[place] = total.astype(bf16)
+    for place, j in enumerate(far_steps + list(ends)):
+        edge_out[place] = pair_sum(0, j).astype(bf16)
         edges[j] = send(edge_out.at[place], edge_in.at[place], hi_partner)
-    reach = nz // 4
+    direct, relayed = {}, {}
+    for number, j in enumerate(near_steps):
+        near_out[number, 0] = pair_sum(0, j).astype(bf16)
+        near_out[number, 1] = pair_sum(1, j).astype(bf16)
+        direct[j] = send(near_out.at[number], near_in.at[number], z_peer[j])
     half = pl.ds(0, 64), pl.ds(64, 64)
 
-    def near_sum(j):
-        place = z_order.index(j)
-        if place // group not in taken:
-            taken.add(place // group)
-            pair_copies[1, place // group].wait_recv()
-        total = term(xh, j, core) + pair_in[1, place].astype(f32)
+    def far_sum(j):
+        total = pair_sum(1, j)
         edges[j].wait_recv()
-        return total + edge_in[place].astype(f32)
-
-    taken = set()
-    direct, relayed = {}, {}
-    far_steps = [j for j in z_far if reach < j < nz - reach]
-    near_steps = [j for j in z_far if j not in far_steps and j not in (reach, nz - reach)]
+        return total + edge_in[(far_steps + list(ends)).index(j)].astype(f32)
+
     for j in far_steps:
-        ring_out[j - 1] = near_sum(j).astype(bf16)
+        ring_out[j - 1] = far_sum(j).astype(bf16)
         if 2 * j == nz:
-            for way, hop in enumerate((reach, nz - reach)):
+            for way, hop in enumerate(ends):
                 relayed[j, way] = send(
                     ring_out.at[j - 1, half[way]], ring_in.at[j - 1, half[way]], z_peer[hop]
                 )
         else:
             hop = j - reach if 2 * j < nz else j + reach
             relayed[j] = send(ring_out.at[j - 1], ring_in.at[j - 1], z_peer[hop])
-    relay_sums = {j: near_sum(j) for j in (reach, nz - reach)}
-    for j in near_steps:
-        ring_out[j - 1] = near_sum(j).astype(bf16)
-        direct[j] = send(ring_out.at[j - 1], ring_in.at[j - 1], z_peer[j])
-    summed = near_sum(0)
-    for way, j in enumerate((reach, nz - reach)):
+    relay_sums = {j: far_sum(j) for j in ends}
+    other, summed = pair_sum(0, 0), pair_sum(1, 0)
+    for number, j in enumerate(near_steps):
+        direct[j].wait_recv()
+        other = other + near_in[number, 0].astype(f32)
+        summed = summed + near_in[number, 1].astype(f32)
+    edge_out[nz - 1] = other.astype(bf16)
+    edges[0] = send(edge_out.at[nz - 1], edge_in.at[nz - 1], hi_partner)
+    for way, j in enumerate(ends):
         total = relay_sums[j]
         for far in far_steps:
             if 2 * far != nz and (2 * far < nz) == (way == 0):
@@ -207,7 +230,9 @@
     back[slots] = jnp.zeros((128, 128), f32)
     for load in loads[5:]:
         load.wait()
-    for j in near_steps + [reach, nz - reach]:
+    edges[0].wait_recv()
+    summed = summed + edge_in[nz - 1].astype(f32)
+    for j in ends:
         direct[j].wait_recv()
         summed = summed + ring_in[j - 1].astype(f32)
 
@@ -224,6 +249,7 @@
         grad_pre, weight, (((1,), (1,)), ((), ())), preferred_element_type=f32
     )
 
+    before_messages = len(started)
     shared = []
 
     def message_at(x_hi, z_at):
@@ -234,7 +260,7 @@
 
     messages[(core * 2 + xh) * nz + z] = message.astype(bf16)
     own = message_at(xh, z)
-    direct = {j: send(own, own, z_peer[j]) for j in (reach, nz - reach)}
+    direct = {j: send(own, own, z_peer[j]) for j in ends}
     swapped = {0: send(own, own, hi_partner)}
     for j in near_steps:
         direct[j] = send(own, own, z_peer[j])
@@ -257,13 +283,14 @@
             parts[core_at, y_at, :, :256] = weight_part[first : first + chunk]
             parts[core_at, y_at, :, 256:] = bias_tile
     pair = send(parts.at[1 - core], parts_in, sibling)
+    drain(before_messages)
     def pass_on(j):
         block = message_at(xh, (z - j) % nz)
         swapped[j] = send(block, block, hi_partner)
         share(block)
 
     relayed = {}
-    for way, j in enumerate((reach, nz - reach)):
+    for way, j in enumerate(ends):
         direct[j].wait_recv()
         place = (core * 2 + xh) * nz + (z - j) % nz
         for hop in range(reach, 0, -1):
@@ -315,11 +342,13 @@
     for copy in x_copies:
         copy.wait_recv()
     z_terms[z] = (x_terms[0] + x_terms[1]) + (x_terms[2] + x_terms[3])
-    z_copies = [send(z_terms.at[z], z_terms.at[z], z_peer[j]) for j in z_far]
+    own = z_terms.at[z]
+    z_copies = {j: send(own, own, z_peer[j]) for j in list(ends) + near_steps}
 
     for copy in shared:
         copy.wait_recv()
 
+    before_back = len(started)
     for slot in range(slots):
         product = jnp.dot(
             masks_t[slot], messages[message_ids[slot]], preferred_element_type=f32
@@ -329,25 +358,39 @@
     def back_term(x_lo, j):
         return back[last[row_of(x_lo, (y + j) % ny)]]
 
-    y_order = y_far + [0]
-    edges = {}
-    for place, j in enumerate(y_order):
+    y_near = (1, ny - 1)
+    y_rest = [j for j in y_far if j not in y_near]
+    edges, direct = {}, {}
+    for place, j in enumerate(y_rest):
         back_edge_out[place] = back_term(1 - xl, j).astype(bf16)
         edges[j] = send(back_edge_out.at[place], back_edge_in.at[place], lo_partner)
-    direct = {}
-    summed = None
-    for place, j in enumerate(y_order):
+    for number, j in enumerate(y_near):
+        beside_out[number, 0] = back_term(1 - xl, j).astype(bf16)
+        beside_out[number, 1] = back_term(xl, j).astype(bf16)
+        direct[j] = send(beside_out.at[number], beside_in.at[number], y_peer[j])
+    for way, j in enumerate(ends):
+        z_copies[j].wait_recv()
+        block = z_terms.at[(z - j) % nz]
+        for hop in range(reach - way, 0, -1):
+            far = reach + hop if way == 0 else nz - reach - hop
+            z_copies[far] = send(block, block, z_peer[hop if way == 0 else nz - hop])
+    for place, j in enumerate(y_rest):
         total = back_term(xl, j)
         edges[j].wait_recv()
         total = total + back_edge_in[place].astype(f32)
-        if j == 0:
-            summed = total
-        else:
-            back_out[j - 1] = total.astype(bf16)
-            direct[j] = send(back_out.at[j - 1], back_in.at[j - 1], y_peer[j])
-
-    for copy in z_copies:
-        copy.wait_recv()
+        back_out[j - 1] = total.astype(bf16)
+        direct[j] = send(back_out.at[j - 1], back_in.at[j - 1], y_peer[j])
+    other, summed = back_term(1 - xl, 0), back_term(xl, 0)
+    for number, j in enumerate(y_near):
+        direct[j].wait_recv()
+        other = other + beside_in[number, 0].astype(f32)
+        summed = summed + beside_in[number, 1].astype(f32)
+    back_edge_out[ny - 1] = other.astype(bf16)
+    edge = send(back_edge_out.at[ny - 1], back_edge_in.at[ny - 1], lo_partner)
+    drain(before_back)
+
+    for j in near_steps + far_steps:
+        z_copies[j].wait_recv()
     total = z_terms[0]
     for z_at in range(1, nz):
         total = total + z_terms[z_at]
@@ -355,7 +398,9 @@
     own = finals.at[core, y]
     y_copies = [send(own, own, y_peer[j]) for j in y_far]
 
-    for j in y_far:
+    edge.wait_recv()
+    summed = summed + back_edge_in[ny - 1].astype(f32)
+    for j in y_rest:
         direct[j].wait_recv()
         summed = summed + back_in[j - 1].astype(f32)
     grad_features_ref[...] = (scale * summed).astype(bf16)
@@ -363,9 +408,8 @@
     for copy in y_copies:
         copy.wait_recv()
     pair = send(finals.at[core], finals.at[core], sibling)
-    for copy in started[:-1]:
-        copy.wait_send()
-    pair.wait()
+    drain(len(started))
+    pair.wait_recv()
     for core_at in (0, 1):
         for y_at in range(ny):
             first = (core_at * ny + y_at) * chunk
@@ -379,8 +423,8 @@
 
 
 def copies_of(ny, nz):
-    forward = (2 * ny - 1) + 2 * (nz // 3) + nz + nz
-    backward = nz + nz + 2 * nz + ny + (ny - 1)
+    forward = (2 * ny - 1) + 2 * (nz // 3) + (nz - 4) + nz
+    backward = nz + nz + 2 * nz + (ny - 2) + (ny - 1)
     weights = 1 + (ny - 1) + 3 + (nz - 1) + (ny - 1) + 1
     return forward + backward + weights
 
@@ -424,12 +468,16 @@
             pltpu.VMEM((slots + 1,) + block, f32),
             pltpu.VMEM((2, nz) + block, bf16),
             pltpu.VMEM((2, nz) + block, bf16),
+            pltpu.VMEM((4, 2) + block, bf16),
+            pltpu.VMEM((4, 2) + block, bf16),
             pltpu.VMEM((nz,) + block, bf16),
             pltpu.VMEM((nz,) + block, bf16),
             pltpu.VMEM((nz - 1,) + block, bf16),
             pltpu.VMEM((nz - 1,) + block, bf16),
             pltpu.VMEM((4 * nz,) + block, bf16),
             pltpu.VMEM((slots + 1,) + block, f32),
+            pltpu.VMEM((2, 2) + block, bf16),
+            pltpu.VMEM((2, 2) + block, bf16),
             pltpu.VMEM((ny,) + block, bf16),
             pltpu.VMEM((ny,) + block, bf16),
             pltpu.VMEM((ny - 1,) + block, bf16),

time: 86.1 us -> 83.6 us (0.971)
  Pallas kernels: 85.3 us -> 82.8 us
    pallas_call x1, Pallas kernels: 83.7 us -> 81.2 us  [on_device(): pl.pallas_call(functools.partial(kernel, ny, nz), out_shape=results, in_s...]
where the time goes in v4:
time: 83.6 us; the launch traced here: 83.5 us
  Pallas kernels  82.8 us (99%)
    pallas_call x1, Pallas kernels, on_device(): pl.pallas_call(functools.partial(kernel, ny, nz), out_shape=results, in_s...  81.2 us

profile of v4, /device:TPU:1, one launch (start us, length us, event | category | flops | bytes accessed | tf_op | source)
XLA Modules:
  0.0 83.5 jit_solution(9526723615662813754)
XLA Ops:
  0.6 81.2 %shard_map.111 = (bf16[128,256]{1,0:T(8,128)(2,1)}, bf16[128,128]{1,0:T(8,128)(2,1)}, f32[128,256]{1,0:T(8,128)}, f32[2,128]{1,0:T(2,128)}) custom-call(bf16[128,128]{1,0:T(8,128)(2,1)} %features_hbm.1, bf16[1,128]{1,0:T(2,128)(2,1)} %bitcast.4, bf16[128,256]{1,0:T(8,128)(2,1)} %weight_hbm.1, f32[1,256]{1,0:T(1,128)} %bitcast.3, s32[1,1,16]{2,1,0:T(1,128)} %rows_hbm.1, ...), custom_call_target="tpu_custom_call" | custom-call | flops 200000000 | bytes 2000000 | tf_op jit(solution)/shard_map/pallas_call | solution.py:447
  81.8 1.7 %shard_map.112 = (bf16[128,256]{1,0:T(8,128)(2,1)}, bf16[128,128]{1,0:T(8,128)(2,1)}, f32[128,256]{1,0:T(8,128)}, f32[2,128]{1,0:T(2,128)}) custom-call(bf16[128,256]{1,0:T(8,128)(2,1)} %get-tuple-element.12.refs_0_, bf16[128,128]{1,0:T(8,128)(2,1)} %get-tuple-element.13.refs_1_, f32[128,256]{1,0:T(8,128)} %get-tuple-element.14.refs_2_, ...), custom_call_target="tpu_custom_call" | custom-call | tf_op jit(solution)/shard_map/pallas_call | solution.py:506

commit v5 on v4

--- a/solution.py
+++ b/solution.py
@@ -284,6 +284,10 @@
             parts[core_at, y_at, :, 256:] = bias_tile
     pair = send(parts.at[1 - core], parts_in, sibling)
     drain(before_messages)
+    pair.wait_recv()
+    halves[...] = parts[core] + parts_in[...]
+    y_copies = {j: send(halves.at[(y + j) % ny], y_in.at[j - 1], y_peer[j]) for j in y_far}
+
     def pass_on(j):
         block = message_at(xh, (z - j) % nz)
         swapped[j] = send(block, block, hi_partner)
@@ -307,35 +311,27 @@
         direct[j].wait_recv()
         pass_on(j)
 
-    pair.wait_recv()
-    halves[...] = parts[core] + parts_in[...]
-    y_copies = {j: send(halves.at[(y + j) % ny], y_in.at[j - 1], y_peer[j]) for j in y_far}
-
-    for j in far_steps[::-1]:
+    for number, j in enumerate(far_steps[::-1]):
         if 2 * j == nz:
             relayed[j, 0].wait_recv()
             relayed[j, 1].wait_recv()
         else:
             relayed[j].wait_recv()
         pass_on(j)
+        if number == 2:
+            total = halves[y]
+            for j in y_far:
+                y_copies[j].wait_recv()
+                total = total + y_in[j - 1]
+            x_at = xh * 2 + xl
+            x_terms[x_at] = total
+            x_copies = [
+                send(x_terms.at[x_at], x_terms.at[x_at], peer)
+                for peer in (lo_partner, hi_partner, far_partner)
+            ]
 
     order = [0, reach, nz - reach] + near_steps
     for j in order:
-        swapped[j].wait_recv()
-        share(message_at(1 - xh, (z - j) % nz))
-
-    total = halves[y]
-    for j in y_far:
-        y_copies[j].wait_recv()
-        total = total + y_in[j - 1]
-    x_at = xh * 2 + xl
-    x_terms[x_at] = total
-    x_copies = [
-        send(x_terms.at[x_at], x_terms.at[x_at], peer)
-        for peer in (lo_partner, hi_partner, far_partner)
-    ]
-
-    for j in far_steps[::-1]:
         swapped[j].wait_recv()
         share(message_at(1 - xh, (z - j) % nz))
 
@@ -344,6 +340,10 @@
     z_terms[z] = (x_terms[0] + x_terms[1]) + (x_terms[2] + x_terms[3])
     own = z_terms.at[z]
     z_copies = {j: send(own, own, z_peer[j]) for j in list(ends) + near_steps}
+
+    for j in far_steps[::-1]:
+        swapped[j].wait_recv()
+        share(message_at(1 - xh, (z - j) % nz))
 
     for copy in shared:
         copy.wait_recv()
@@ -374,6 +374,7 @@
         for hop in range(reach - way, 0, -1):
             far = reach + hop if way == 0 else nz - reach - hop
             z_copies[far] = send(block, block, z_peer[hop if way == 0 else nz - hop])
+
     for place, j in enumerate(y_rest):
         total = back_term(xl, j)
         edges[j].wait_recv()
@@ -400,14 +401,15 @@
 
     edge.wait_recv()
     summed = summed + back_edge_in[ny - 1].astype(f32)
-    for j in y_rest:
-        direct[j].wait_recv()
-        summed = summed + back_in[j - 1].astype(f32)
-    grad_features_ref[...] = (scale * summed).astype(bf16)
-
     for copy in y_copies:
         copy.wait_recv()
     pair = send(finals.at[core], finals.at[core], sibling)
+
+    for j in y_rest:
+        direct[j].wait_recv()
+        summed = summed + back_in[j - 1].astype(f32)
+    grad_features_ref[...] = (scale * summed).astype(bf16)
+
     drain(len(started))
     pair.wait_recv()
     for core_at in (0, 1):

time: 83.6 us -> 82.8 us (level)
  no operation moved by 1% of the time
where the time goes in v5:
time: 82.8 us; the launch traced here: 82.7 us
  Pallas kernels  82 us (99%)
    pallas_call x1, Pallas kernels, on_device(): pl.pallas_call(functools.partial(kernel, ny, nz), out_shape=results, in_s...  80.4 us
    pallas_call x1, Pallas kernels, on_device(): pl.pallas_call(store, out_shape=results, in_specs=[vmem] * 4, out_specs=(...  1.66 us

profile of v5, /device:TPU:1, one launch (start us, length us, event | category | flops | bytes accessed | tf_op | source)
XLA Modules:
  0.0 82.7 jit_solution(6113284413471854581)
XLA Ops:
  0.6 80.4 %shard_map.111 = (bf16[128,256]{1,0:T(8,128)(2,1)}, bf16[128,128]{1,0:T(8,128)(2,1)}, f32[128,256]{1,0:T(8,128)}, f32[2,128]{1,0:T(2,128)}) custom-call(bf16[128,128]{1,0:T(8,128)(2,1)} %features_hbm.1, bf16[1,128]{1,0:T(2,128)(2,1)} %bitcast.4, bf16[128,256]{1,0:T(8,128)(2,1)} %weight_hbm.1, f32[1,256]{1,0:T(1,128)} %bitcast.3, s32[1,1,16]{2,1,0:T(1,128)} %rows_hbm.1, ...), custom_call_target="tpu_custom_call" | custom-call | flops 200000000 | bytes 2000000 | tf_op jit(solution)/shard_map/pallas_call | solution.py:449
  81.0 1.7 %shard_map.112 = (bf16[128,256]{1,0:T(8,128)(2,1)}, bf16[128,128]{1,0:T(8,128)(2,1)}, f32[128,256]{1,0:T(8,128)}, f32[2,128]{1,0:T(2,128)}) custom-call(bf16[128,256]{1,0:T(8,128)(2,1)} %get-tuple-element.12.refs_0_, bf16[128,128]{1,0:T(8,128)(2,1)} %get-tuple-element.13.refs_1_, f32[128,256]{1,0:T(8,128)} %get-tuple-element.14.refs_2_, ...), custom_call_target="tpu_custom_call" | custom-call | tf_op jit(solution)/shard_map/pallas_call | solution.py:508

commit v6 on v4

--- a/solution.py
+++ b/solution.py
@@ -134,7 +134,7 @@
         return products[owners[col_of(x_hi, (z + j) % nz, core_at)]]
 
     z_order = z_far + [0]
-    group = 3
+    group = 2
     pair_copies = {}
     for piece, x_hi in enumerate((1 - xh, xh)):
         for place, j in enumerate(z_order):
@@ -423,7 +423,7 @@
 
 
 def copies_of(ny, nz):
-    forward = (2 * ny - 1) + 2 * (nz // 3) + (nz - 4) + nz
+    forward = (2 * ny - 1) + 2 * (nz // 2) + (nz - 4) + nz
     backward = nz + nz + 2 * nz + (ny - 2) + (ny - 1)
     weights = 1 + (ny - 1) + 3 + (nz - 1) + (ny - 1) + 1
     return forward + backward + weights

time: 83.6 us -> 83.8 us (level)
  no operation moved by 1% of the time
where the time goes in v6:
time: 83.8 us; the launch traced here: 83.7 us
  Pallas kernels  83.1 us (99%)
    pallas_call x1, Pallas kernels, on_device(): pl.pallas_call(functools.partial(kernel, ny, nz), out_shape=results, in_s...  81.4 us

profile of v6, /device:TPU:1, one launch (start us, length us, event | category | flops | bytes accessed | tf_op | source)
XLA Modules:
  0.0 83.7 jit_solution(2431741127292735616)
XLA Ops:
  0.6 81.4 %shard_map.111 = (bf16[128,256]{1,0:T(8,128)(2,1)}, bf16[128,128]{1,0:T(8,128)(2,1)}, f32[128,256]{1,0:T(8,128)}, f32[2,128]{1,0:T(2,128)}) custom-call(bf16[128,128]{1,0:T(8,128)(2,1)} %features_hbm.1, bf16[1,128]{1,0:T(2,128)(2,1)} %bitcast.4, bf16[128,256]{1,0:T(8,128)(2,1)} %weight_hbm.1, f32[1,256]{1,0:T(1,128)} %bitcast.3, s32[1,1,16]{2,1,0:T(1,128)} %rows_hbm.1, ...), custom_call_target="tpu_custom_call" | custom-call | flops 200000000 | bytes 2000000 | tf_op jit(solution)/shard_map/pallas_call | solution.py:447
  82.1 1.7 %shard_map.112 = (bf16[128,256]{1,0:T(8,128)(2,1)}, bf16[128,128]{1,0:T(8,128)(2,1)}, f32[128,256]{1,0:T(8,128)}, f32[2,128]{1,0:T(2,128)}) custom-call(bf16[128,256]{1,0:T(8,128)(2,1)} %get-tuple-element.12.refs_0_, bf16[128,128]{1,0:T(8,128)(2,1)} %get-tuple-element.13.refs_1_, f32[128,256]{1,0:T(8,128)} %get-tuple-element.14.refs_2_, ...), custom_call_target="tpu_custom_call" | custom-call | tf_op jit(solution)/shard_map/pallas_call | solution.py:506
